TPU v7x, 256 devices: a whole 4x4x8 slice. The times are simulated.
256 devices in a mesh: tm: 8 (over y, core), mp: 4 (over z_lo), tok: 8 (over z_hi, x).
Axes of the slice: x: 4, y: 4, z: 8 (z_hi: 2, z_lo: 4; z = z_hi * 4 + z_lo), core: 2. Of those that a mesh axis runs over, the one named last changes fastest.
Arguments:
- features: bfloat16 [1024, 3584], P('tok'), may hold values from -6 to 6
- spike_mask: int32 [8, 1024, 3584], P('tm', 'tok'), may hold values 0 or 1
- gate_weight: bfloat16 [3584, 7168], P(('tm', 'tok'), 'mp'), may hold values from -0.09375 to 0.09375
- threshold: float32 [7168], P('mp'), may hold values from 0.5 to 2
Outputs:
- rates: float32 [1024, 7168], P('tok', 'mp')
- grad_threshold: float32 [7168], P('mp')
All inputs are finite; a program needn't handle non-finite values. No bound on the sum of `spike_mask` on one device may be relied on, other than what follows from the above.
Results may differ from a plain program's by a relative error of at most 0.00035.
Values may be sent and summed in bfloat16 or wider, within the bound.
No kernel may reach another device: no remote copies, remote signals or barrier semaphores. Data moves between devices by JAX's collectives and lax.ppermute only.
A program may use at most 64 MiB of HBM per device.

v0:
```python
import jax
import jax.numpy as jnp
from jax import lax
from jax.sharding import PartitionSpec as P

SHARP = 2.0


def passed_along(x, axis, by):
    peers = lax.axis_size(axis)
    pairs = [(i, i + by) for i in range(peers) if 0 <= i + by < peers]
    return lax.ppermute(x, axis, pairs)


def on_device(features, spike_mask, gate_weight, threshold):
    steps = lax.axis_size("tm")
    step_index = lax.axis_index("tm")
    tokens_all = features.shape[0] * lax.axis_size("tok")
    rows = features.shape[0]
    width = gate_weight.shape[1]
    driven = jnp.where(spike_mask[0] > 0, features, jnp.zeros_like(features))
    piece = lax.all_gather(gate_weight, ("tm", "tok"), axis=0, tiled=True)
    student = jnp.dot(driven, piece, preferred_element_type=jnp.float32)
    teacher = jnp.dot(features, piece, preferred_element_type=jnp.float32)
    current = 2.0 * student
    target = jax.nn.silu(teacher)
    blocks = 1
    size = rows // blocks
    turns = steps + blocks - 1

    def forward_turn(turn, carry):
        incoming, spikes = carry
        block = turn - step_index
        active = (block >= 0) & (block < blocks)
        rising = incoming + current
        fired = jax.nn.sigmoid(SHARP * (rising - threshold))
        leaving = rising - threshold * fired
        older = spikes
        spikes = jnp.where(active, fired, older)
        passed = passed_along(leaving, "tm", 1)
        return (passed, spikes)

    block_zero = jnp.zeros((size, width), jnp.float32)
    unused, spikes = lax.fori_loop(
        0, turns, forward_turn, (block_zero, jnp.zeros((rows, width), jnp.float32))
    )
    total = lax.psum(spikes, "tm")
    rates = threshold * total / steps
    error = (rates - target) / tokens_all

    def backward_turn(turn, carry):
        incoming, grad_sum = carry
        block = turn - (steps - 1 - step_index)
        active = (block >= 0) & (block < blocks)
        dspike = error * threshold / steps - threshold * incoming
        dwide = dspike * SHARP * spikes * (1.0 - spikes)
        term = jnp.sum(-dwide - spikes * incoming + error * spikes / steps, axis=0)
        grad_sum = grad_sum + jnp.where(active, term, jnp.zeros_like(term))
        passed = passed_along((incoming + dwide).astype(jnp.bfloat16), "tm", -1).astype(jnp.float32)
        return (passed, grad_sum)

    unused_cot, grad_local = lax.fori_loop(
        0, turns, backward_turn, (block_zero, jnp.zeros((width,), jnp.float32))
    )
    grad_threshold = lax.psum(grad_local, ("tm", "tok"))
    return (rates, grad_threshold)


def solution(mesh):
    return jax.shard_map(
        on_device,
        mesh=mesh,
        in_specs=(P("tok", None), P("tm", "tok", None), P(("tm", "tok"), "mp"), P("mp")),
        out_specs=(P("tok", "mp"), P("mp")),
        check_vma=False,
    )
```

profile of v0, /device:TPU:32, one launch (start us, length us, event | category | flops | bytes accessed | tf_op | source)
XLA Modules:
  0.0 676.2 jit_solution(10581541776726929995)
XLA Ops:
  8.0 140.1 %all-gather.2.cloned.1.call-done = bf16[3584,1792]{1,0:T(8,128)(2,1)} async-done(((bf16[56,1792]{1,0:T(8,128)(2,1)}), bf16[3584,1792]{1,0:T(8,128)(2,1)}) %all-gather.2.cloned.1.call-update) | async-done | bytes 12845072 | tf_op jit(solution)/shard_map/all_gather | solution.py:22
  148.0 7.4 %convolution_multiply_fusion = f32[128,1792]{1,0:T(8,128)S(1)} fusion(bf16[3584,1792]{1,0:T(8,128)(2,1)} %all-gather.2.cloned.1.call-done, bf16[128,3584]{1,0:T(8,128)(2,1)} %param.8, s32[1,128,3584]{2,1,0:T(8,128)} %param.9), kind=kOutput, calls=%fused_computation.8 | convolution fusion | flops 1645314048 | bytes 16515072 | tf_op jit(solution)/shard_map/dot_general | solution.py:23
  155.5 120.2 %while.34 = (s32[]{:T(128)}, f32[128,1792]{1,0:T(8,128)S(1)}, f32[128,1792]{1,0:T(8,128)S(1)}, f32[128,1792]{1,0:T(8,128)S(1)}, f32[1792]{0:T(1024)S(1)}, /*index=5*/s32[]{:T(128)}, s32[]{:T(128)}, s32[]{:T(128)}) while((s32[]{:T(128)}, f32[128,1792]{1,0:T(8,128)S(1)}, f32[128,1792]{1,0:T(8,128)S(1)}, f32[128,1792]{1,0:T(8,128)S(1)}, ...), condition=%wide.region_1.2_spmd.clone, body=%wide.region_0.1_spmd.clone.sunk | while | flops 2293767 | bytes 8264873 | solution.py:44
  157.1 2.2 collective-permute-start
  159.3 2.2 collective-permute-done
  163.1 11.6 %collective-permute-start = (f32[128,1792]{1,0:T(8,128)}, f32[128,1792]{1,0:T(8,128)S(1)}, u32[]{:S(2)}, u32[]{:S(2)}) collective-permute-start(f32[128,1792]{1,0:T(8,128)} %get-tuple-element.455), channel_id=1, source_target_pairs={{0,32},{32,64},{64,96},{96,128},{128,160},{160,192},{192,224},{1,3... | collective-permute-start | bytes 2752520 | tf_op jit(solution)/shard_map/while/body/eval_jaxpr/ppermute | solution.py:12
  174.7 2.2 collective-permute-done
  178.4 12.7 %collective-permute-start = (f32[128,1792]{1,0:T(8,128)}, f32[128,1792]{1,0:T(8,128)S(1)}, u32[]{:S(2)}, u32[]{:S(2)}) collective-permute-start(f32[128,1792]{1,0:T(8,128)} %get-tuple-element.455), channel_id=1, source_target_pairs={{0,32},{32,64},{64,96},{96,128},{128,160},{160,192},{192,224},{1,3... | collective-permute-start | bytes 2752520 | tf_op jit(solution)/shard_map/while/body/eval_jaxpr/ppermute | solution.py:12
  191.1 2.2 collective-permute-done
  194.9 12.7 %collective-permute-start = (f32[128,1792]{1,0:T(8,128)}, f32[128,1792]{1,0:T(8,128)S(1)}, u32[]{:S(2)}, u32[]{:S(2)}) collective-permute-start(f32[128,1792]{1,0:T(8,128)} %get-tuple-element.455), channel_id=1, source_target_pairs={{0,32},{32,64},{64,96},{96,128},{128,160},{160,192},{192,224},{1,3... | collective-permute-start | bytes 2752520 | tf_op jit(solution)/shard_map/while/body/eval_jaxpr/ppermute | solution.py:12
  207.6 2.2 collective-permute-done
  211.4 12.7 %collective-permute-start = (f32[128,1792]{1,0:T(8,128)}, f32[128,1792]{1,0:T(8,128)S(1)}, u32[]{:S(2)}, u32[]{:S(2)}) collective-permute-start(f32[128,1792]{1,0:T(8,128)} %get-tuple-element.455), channel_id=1, source_target_pairs={{0,32},{32,64},{64,96},{96,128},{128,160},{160,192},{192,224},{1,3... | collective-permute-start | bytes 2752520 | tf_op jit(solution)/shard_map/while/body/eval_jaxpr/ppermute | solution.py:12
  224.0 2.2 collective-permute-done
  227.8 12.7 %collective-permute-start = (f32[128,1792]{1,0:T(8,128)}, f32[128,1792]{1,0:T(8,128)S(1)}, u32[]{:S(2)}, u32[]{:S(2)}) collective-permute-start(f32[128,1792]{1,0:T(8,128)} %get-tuple-element.455), channel_id=1, source_target_pairs={{0,32},{32,64},{64,96},{96,128},{128,160},{160,192},{192,224},{1,3... | collective-permute-start | bytes 2752520 | tf_op jit(solution)/shard_map/while/body/eval_jaxpr/ppermute | solution.py:12
  240.5 2.2 collective-permute-done
  244.3 12.7 %collective-permute-start = (f32[128,1792]{1,0:T(8,128)}, f32[128,1792]{1,0:T(8,128)S(1)}, u32[]{:S(2)}, u32[]{:S(2)}) collective-permute-start(f32[128,1792]{1,0:T(8,128)} %get-tuple-element.455), channel_id=1, source_target_pairs={{0,32},{32,64},{64,96},{96,128},{128,160},{160,192},{192,224},{1,3... | collective-permute-start | bytes 2752520 | tf_op jit(solution)/shard_map/while/body/eval_jaxpr/ppermute | solution.py:12
  256.9 2.2 collective-permute-done
  260.7 12.7 %collective-permute-start = (f32[128,1792]{1,0:T(8,128)}, f32[128,1792]{1,0:T(8,128)S(1)}, u32[]{:S(2)}, u32[]{:S(2)}) collective-permute-start(f32[128,1792]{1,0:T(8,128)} %get-tuple-element.455), channel_id=1, source_target_pairs={{0,32},{32,64},{64,96},{96,128},{128,160},{160,192},{192,224},{1,3... | collective-permute-start | bytes 2752520 | tf_op jit(solution)/shard_map/while/body/eval_jaxpr/ppermute | solution.py:12
  273.4 2.2 collective-permute-done
  276.7 74.4 %all-reduce.2.cloned.1.call-done = f32[128,1792]{1,0:T(8,128)} async-done(((f32[128,1792]{1,0:T(8,128)}), f32[128,1792]{1,0:T(8,128)}) %all-reduce.2.cloned.1.call-update) | async-done | bytes 917520 | tf_op jit(solution)/shard_map/psum | solution.py:47
  351.1 8.4 %fusion.4 = (f32[128,1792]{1,0:T(8,128)S(1)}, f32[128,1792]{1,0:T(8,128)S(1)}, f32[128,1792]{1,0:T(8,128)}) fusion(f32[128,1792]{1,0:T(8,128)} %copy-done, f32[128,1792]{1,0:T(8,128)} %all-reduce.2.cloned.1.call-done, f32[1792]{0:T(1024)S(1)} %get-tuple-element.528, bf16[128,3584]{1,0:T(8,128)(2,1)} %param.8, ...), kind=kOutput, calls=%fused_computation.16 | convolution fusion | flops 1646231552 | bytes 18357248 | tf_op jit(solution)/shard_map/dot_general | solution.py:24
  359.4 99.1 %while.35 = (s32[]{:T(128)}, f32[128,1792]{1,0:T(8,128)}, f32[1792]{0:T(1024)S(1)}, f32[1792]{0:T(1024)S(1)}, f32[128,1792]{1,0:T(8,128)S(1)}, /*index=5*/f32[12...) while((s32[]{:T(128)}, f32[128,1792]{1,0:T(8,128)}, ...), condition=%wide.region_5.6_spmd.clone, body=%wide.region_3.5_spmd.clone.sunk | while | flops 4132359 | bytes 7376058 | solution.py:62
  361.3 2.5 collective-permute-done.1
  363.8 2.0 convert_element_type.22
  368.8 5.9 collective-permute-done.1
  379.8 8.6 %collective-permute-done.1 = bf16[128,1792]{1,0:T(8,128)(2,1)} collective-permute-done((bf16[128,1792]{1,0:T(8,128)(2,1)S(1)}, bf16[128,1792]{1,0:T(8,128)(2,1)}, u32[]{:S(2)}, u32[]{:S(2)}) %collective-permute-start.1) | collective-permute-done | bytes 458784 | tf_op jit(solution)/shard_map/while/body/eval_jaxpr/ppermute | solution.py:12
  393.4 8.6 %collective-permute-done.1 = bf16[128,1792]{1,0:T(8,128)(2,1)} collective-permute-done((bf16[128,1792]{1,0:T(8,128)(2,1)S(1)}, bf16[128,1792]{1,0:T(8,128)(2,1)}, u32[]{:S(2)}, u32[]{:S(2)}) %collective-permute-start.1) | collective-permute-done | bytes 458784 | tf_op jit(solution)/shard_map/while/body/eval_jaxpr/ppermute | solution.py:12
  407.0 8.6 %collective-permute-done.1 = bf16[128,1792]{1,0:T(8,128)(2,1)} collective-permute-done((bf16[128,1792]{1,0:T(8,128)(2,1)S(1)}, bf16[128,1792]{1,0:T(8,128)(2,1)}, u32[]{:S(2)}, u32[]{:S(2)}) %collective-permute-start.1) | collective-permute-done | bytes 458784 | tf_op jit(solution)/shard_map/while/body/eval_jaxpr/ppermute | solution.py:12
  420.7 8.6 %collective-permute-done.1 = bf16[128,1792]{1,0:T(8,128)(2,1)} collective-permute-done((bf16[128,1792]{1,0:T(8,128)(2,1)S(1)}, bf16[128,1792]{1,0:T(8,128)(2,1)}, u32[]{:S(2)}, u32[]{:S(2)}) %collective-permute-start.1) | collective-permute-done | bytes 458784 | tf_op jit(solution)/shard_map/while/body/eval_jaxpr/ppermute | solution.py:12
  434.3 8.6 %collective-permute-done.1 = bf16[128,1792]{1,0:T(8,128)(2,1)} collective-permute-done((bf16[128,1792]{1,0:T(8,128)(2,1)S(1)}, bf16[128,1792]{1,0:T(8,128)(2,1)}, u32[]{:S(2)}, u32[]{:S(2)}) %collective-permute-start.1) | collective-permute-done | bytes 458784 | tf_op jit(solution)/shard_map/while/body/eval_jaxpr/ppermute | solution.py:12
  447.9 8.6 %collective-permute-done.1 = bf16[128,1792]{1,0:T(8,128)(2,1)} collective-permute-done((bf16[128,1792]{1,0:T(8,128)(2,1)S(1)}, bf16[128,1792]{1,0:T(8,128)(2,1)}, u32[]{:S(2)}, u32[]{:S(2)}) %collective-permute-start.1) | collective-permute-done | bytes 458784 | tf_op jit(solution)/shard_map/while/body/eval_jaxpr/ppermute | solution.py:12
  458.5 210.8 %psum.15 = f32[1792]{0:T(1024)} all-reduce(f32[1792]{0:T(1024)S(1)} %get-tuple-element.289), channel_id=1, replica_groups=mesh['tm'=8,'mp'=4,'tok'=8] {'tm','tok'}, use_global_device_ids=true, to_apply=%region_6.7 | all-reduce | flops 1792 | bytes 14336 | tf_op jit(solution)/shard_map/psum | solution.py:65
  (53 shorter events, 51.1 us)
Async XLA Ops:
  7.2 140.9 %all-gather.2.cloned.1.call-start = ((), (), s32[]{:S(2)}) async-start(), calls=%async_computation | async-start | bytes 13045760 | tf_op jit(solution)/shard_map/all_gather | solution.py:22
  7.9 343.2 %all-reduce.2.cloned.1.call-start = ((), (), s32[]{:S(2)}) async-start(), calls=%async_computation.1 | async-start | bytes 1835008 | tf_op jit(solution)/shard_map/psum | solution.py:47
  8.0 147.5 %copy-start.2 = (f32[1792]{0:T(1024)S(1)}, f32[1792]{0:T(1024)}, u32[]{:S(2)}) copy-start(f32[1792]{0:T(1024)} %param.11) | copy-start | bytes 21508
  157.1 4.5 collective-permute-start
  163.1 13.8 %collective-permute-start = (f32[128,1792]{1,0:T(8,128)}, f32[128,1792]{1,0:T(8,128)S(1)}, u32[]{:S(2)}, u32[]{:S(2)}) collective-permute-start(f32[128,1792]{1,0:T(8,128)} %get-tuple-element.455), channel_id=1, source_target_pairs={{0,32},{32,64},{64,96},{96,128},{128,160},{160,192},{192,224},{1,3... | collective-permute-start | bytes 2752520 | tf_op jit(solution)/shard_map/while/body/eval_jaxpr/ppermute | solution.py:12
  178.4 14.9 %collective-permute-start = (f32[128,1792]{1,0:T(8,128)}, f32[128,1792]{1,0:T(8,128)S(1)}, u32[]{:S(2)}, u32[]{:S(2)}) collective-permute-start(f32[128,1792]{1,0:T(8,128)} %get-tuple-element.455), channel_id=1, source_target_pairs={{0,32},{32,64},{64,96},{96,128},{128,160},{160,192},{192,224},{1,3... | collective-permute-start | bytes 2752520 | tf_op jit(solution)/shard_map/while/body/eval_jaxpr/ppermute | solution.py:12
  194.9 14.9 %collective-permute-start = (f32[128,1792]{1,0:T(8,128)}, f32[128,1792]{1,0:T(8,128)S(1)}, u32[]{:S(2)}, u32[]{:S(2)}) collective-permute-start(f32[128,1792]{1,0:T(8,128)} %get-tuple-element.455), channel_id=1, source_target_pairs={{0,32},{32,64},{64,96},{96,128},{128,160},{160,192},{192,224},{1,3... | collective-permute-start | bytes 2752520 | tf_op jit(solution)/shard_map/while/body/eval_jaxpr/ppermute | solution.py:12
  211.4 14.9 %collective-permute-start = (f32[128,1792]{1,0:T(8,128)}, f32[128,1792]{1,0:T(8,128)S(1)}, u32[]{:S(2)}, u32[]{:S(2)}) collective-permute-start(f32[128,1792]{1,0:T(8,128)} %get-tuple-element.455), channel_id=1, source_target_pairs={{0,32},{32,64},{64,96},{96,128},{128,160},{160,192},{192,224},{1,3... | collective-permute-start | bytes 2752520 | tf_op jit(solution)/shard_map/while/body/eval_jaxpr/ppermute | solution.py:12
  227.8 14.9 %collective-permute-start = (f32[128,1792]{1,0:T(8,128)}, f32[128,1792]{1,0:T(8,128)S(1)}, u32[]{:S(2)}, u32[]{:S(2)}) collective-permute-start(f32[128,1792]{1,0:T(8,128)} %get-tuple-element.455), channel_id=1, source_target_pairs={{0,32},{32,64},{64,96},{96,128},{128,160},{160,192},{192,224},{1,3... | collective-permute-start | bytes 2752520 | tf_op jit(solution)/shard_map/while/body/eval_jaxpr/ppermute | solution.py:12
  244.3 14.9 %collective-permute-start = (f32[128,1792]{1,0:T(8,128)}, f32[128,1792]{1,0:T(8,128)S(1)}, u32[]{:S(2)}, u32[]{:S(2)}) collective-permute-start(f32[128,1792]{1,0:T(8,128)} %get-tuple-element.455), channel_id=1, source_target_pairs={{0,32},{32,64},{64,96},{96,128},{128,160},{160,192},{192,224},{1,3... | collective-permute-start | bytes 2752520 | tf_op jit(solution)/shard_map/while/body/eval_jaxpr/ppermute | solution.py:12
  260.7 14.9 %collective-permute-start = (f32[128,1792]{1,0:T(8,128)}, f32[128,1792]{1,0:T(8,128)S(1)}, u32[]{:S(2)}, u32[]{:S(2)}) collective-permute-start(f32[128,1792]{1,0:T(8,128)} %get-tuple-element.455), channel_id=1, source_target_pairs={{0,32},{32,64},{64,96},{96,128},{128,160},{160,192},{192,224},{1,3... | collective-permute-start | bytes 2752520 | tf_op jit(solution)/shard_map/while/body/eval_jaxpr/ppermute | solution.py:12
  275.6 1.0 copy-start
  276.7 82.8 %copy-start.1 = (f32[128,1792]{1,0:T(8,128)S(1)}, f32[128,1792]{1,0:T(8,128)}, u32[]{:S(2)}) copy-start(f32[128,1792]{1,0:T(8,128)} %copy-done) | copy-start | bytes 2752516
  360.0 3.8 collective-permute-start.1
  367.5 7.2 %collective-permute-start.1 = (bf16[128,1792]{1,0:T(8,128)(2,1)S(1)}, bf16[128,1792]{1,0:T(8,128)(2,1)}, u32[]{:S(2)}, u32[]{:S(2)}) collective-permute-start(bf16[128,1792]{1,0:T(8,128)(2,1)S(1)} %get-tuple-element.465), channel_id=1, source_target_pairs={{32,0},{64,32},{96,64},{128,96},{160,128},{192,160},{224,192},{33,... | collective-permute-start | bytes 1376264 | tf_op jit(solution)/shard_map/while/body/eval_jaxpr/ppermute | solution.py:12
  378.5 9.9 %collective-permute-start.1 = (bf16[128,1792]{1,0:T(8,128)(2,1)S(1)}, bf16[128,1792]{1,0:T(8,128)(2,1)}, u32[]{:S(2)}, u32[]{:S(2)}) collective-permute-start(bf16[128,1792]{1,0:T(8,128)(2,1)S(1)} %get-tuple-element.465), channel_id=1, source_target_pairs={{32,0},{64,32},{96,64},{128,96},{160,128},{192,160},{224,192},{33,... | collective-permute-start | bytes 1376264 | tf_op jit(solution)/shard_map/while/body/eval_jaxpr/ppermute | solution.py:12
  392.1 9.9 %collective-permute-start.1 = (bf16[128,1792]{1,0:T(8,128)(2,1)S(1)}, bf16[128,1792]{1,0:T(8,128)(2,1)}, u32[]{:S(2)}, u32[]{:S(2)}) collective-permute-start(bf16[128,1792]{1,0:T(8,128)(2,1)S(1)} %get-tuple-element.465), channel_id=1, source_target_pairs={{32,0},{64,32},{96,64},{128,96},{160,128},{192,160},{224,192},{33,... | collective-permute-start | bytes 1376264 | tf_op jit(solution)/shard_map/while/body/eval_jaxpr/ppermute | solution.py:12
  405.7 9.9 %collective-permute-start.1 = (bf16[128,1792]{1,0:T(8,128)(2,1)S(1)}, bf16[128,1792]{1,0:T(8,128)(2,1)}, u32[]{:S(2)}, u32[]{:S(2)}) collective-permute-start(bf16[128,1792]{1,0:T(8,128)(2,1)S(1)} %get-tuple-element.465), channel_id=1, source_target_pairs={{32,0},{64,32},{96,64},{128,96},{160,128},{192,160},{224,192},{33,... | collective-permute-start | bytes 1376264 | tf_op jit(solution)/shard_map/while/body/eval_jaxpr/ppermute | solution.py:12
  419.3 9.9 %collective-permute-start.1 = (bf16[128,1792]{1,0:T(8,128)(2,1)S(1)}, bf16[128,1792]{1,0:T(8,128)(2,1)}, u32[]{:S(2)}, u32[]{:S(2)}) collective-permute-start(bf16[128,1792]{1,0:T(8,128)(2,1)S(1)} %get-tuple-element.465), channel_id=1, source_target_pairs={{32,0},{64,32},{96,64},{128,96},{160,128},{192,160},{224,192},{33,... | collective-permute-start | bytes 1376264 | tf_op jit(solution)/shard_map/while/body/eval_jaxpr/ppermute | solution.py:12
  433.0 9.9 %collective-permute-start.1 = (bf16[128,1792]{1,0:T(8,128)(2,1)S(1)}, bf16[128,1792]{1,0:T(8,128)(2,1)}, u32[]{:S(2)}, u32[]{:S(2)}) collective-permute-start(bf16[128,1792]{1,0:T(8,128)(2,1)S(1)} %get-tuple-element.465), channel_id=1, source_target_pairs={{32,0},{64,32},{96,64},{128,96},{160,128},{192,160},{224,192},{33,... | collective-permute-start | bytes 1376264 | tf_op jit(solution)/shard_map/while/body/eval_jaxpr/ppermute | solution.py:12
  446.6 9.9 %collective-permute-start.1 = (bf16[128,1792]{1,0:T(8,128)(2,1)S(1)}, bf16[128,1792]{1,0:T(8,128)(2,1)}, u32[]{:S(2)}, u32[]{:S(2)}) collective-permute-start(bf16[128,1792]{1,0:T(8,128)(2,1)S(1)} %get-tuple-element.465), channel_id=1, source_target_pairs={{32,0},{64,32},{96,64},{128,96},{160,128},{192,160},{224,192},{33,... | collective-permute-start | bytes 1376264 | tf_op jit(solution)/shard_map/while/body/eval_jaxpr/ppermute | solution.py:12
Sparse Core Ops, SparseCore 0:
  11.7 136.3 all-gather.1
  276.8 74.2 all-reduce.1
where the time goes:
time: 677 us; the launch traced here: 676 us
  waiting for transfers between devices  293 us (43%)
  blocking collectives  211 us (31%)
  starting transfers between devices  100 us (15%)
  other arithmetic  41 us (6%)
  matrix products  15.7 us (2%)
  between operations  14.1 us (2%)
    psum x1, blocking collectives, on_device(): grad_threshold = lax.psum(grad_local, ('tm', 'tok'))  211 us
    all_gather x1, waiting for transfers between devices, on_device(): piece = lax.all_gather(gate_weight, ('tm', 'tok'), axis=0, tiled=True)  140 us
    ppermute x16, starting transfers between devices, passed_along(): return lax.ppermute(x, axis, pairs)  100 us
    ppermute x16, waiting for transfers between devices, passed_along(): return lax.ppermute(x, axis, pairs)  77.7 us
    psum x1, waiting for transfers between devices, on_device(): total = lax.psum(spikes, 'tm')  74.4 us
    convert_element_type x8, other arithmetic, backward_turn(): passed_along((incoming + dwide).astype(jnp.bfloat16), 'tm', -1)  16.3 us
  transfers between devices with their start and end apart: 18, of which 18 were waited for; matrix products, arithmetic and copies ran while one was open for 0% of the time, Pallas kernels for 0%

commit v1 on v0

--- a/solution.py
+++ b/solution.py
@@ -19,7 +19,10 @@
     rows = features.shape[0]
     width = gate_weight.shape[1]
     driven = jnp.where(spike_mask[0] > 0, features, jnp.zeros_like(features))
-    piece = lax.all_gather(gate_weight, ("tm", "tok"), axis=0, tiled=True)
+    peers_2 = lax.axis_size(("tm", "tok"))
+    pieces = jnp.stack([gate_weight for _ in range(peers_2)])
+    pieces = lax.all_to_all(pieces, ("tm", "tok"), split_axis=0, concat_axis=0)
+    piece = jnp.concatenate(pieces, axis=0)
     student = jnp.dot(driven, piece, preferred_element_type=jnp.float32)
     teacher = jnp.dot(features, piece, preferred_element_type=jnp.float32)
     current = 2.0 * student

time: 677 us -> 882 us (1.30)
  waiting for transfers between devices: 293 us -> 484 us
    all_to_all x0 -> x1, waiting for transfers between devices: none -> 288 us  [on_device(): pieces = lax.all_to_all(pieces, ('tm', 'tok'), split_axis=0, concat_axis=0)]
    all_gather x1 -> x0, waiting for transfers between devices: 140 us -> none  [on_device(): piece = lax.all_gather(gate_weight, ('tm', 'tok'), axis=0, tiled=True)]
    psum x1, waiting for transfers between devices: 74.4 us -> 118 us  [on_device(): total = lax.psum(spikes, 'tm')]
    all_to_all x0 -> x1, starting transfers between devices: none -> 14 us  [on_device(): pieces = lax.all_to_all(pieces, ('tm', 'tok'), split_axis=0, concat_axis=0)]
where the time goes in v1:
time: 882 us; the launch traced here: 881 us
  waiting for transfers between devices  484 us (55%)
  blocking collectives  211 us (24%)
  starting transfers between devices  108 us (12%)
  other arithmetic  41 us (5%)
  matrix products  15.5 us (2%)
  between operations  14.1 us (2%)
    all_to_all x1, waiting for transfers between devices, on_device(): pieces = lax.all_to_all(pieces, ('tm', 'tok'), split_axis=0, concat_axis=0)  288 us
    psum x1, blocking collectives, on_device(): grad_threshold = lax.psum(grad_local, ('tm', 'tok'))  211 us
    psum x1, waiting for transfers between devices, on_device(): total = lax.psum(spikes, 'tm')  118 us
    ppermute x16, starting transfers between devices, passed_along(): return lax.ppermute(x, axis, pairs)  93.5 us
    ppermute x16, waiting for transfers between devices, passed_along(): return lax.ppermute(x, axis, pairs)  77.7 us
  transfers between devices with their start and end apart: 18, of which 18 were waited for; matrix products, arithmetic and copies ran while one was open for 0% of the time, Pallas kernels for 0%

profile of v1, /device:TPU:32, one launch (start us, length us, event | category | flops | bytes accessed | tf_op | source)
XLA Modules:
  0.0 880.5 jit_solution(4498688554805008026)
XLA Ops:
  7.2 6.4 stack.2
  13.5 14.0 %all-to-all-start = ((bf16[64,56,1792]{2,1,0:T(8,128)(2,1)}), bf16[64,56,1792]{2,1,0:T(8,128)(2,1)}, u32[]{:S(2)}, u32[]{:S(2)}) async-start(bf16[64,56,1792]{2,1,0:T(8,128)(2,1)} %stack.2), calls=%async_computation | async-start | bytes 25690112 | tf_op jit(solution)/shard_map/all_to_all | solution.py:24
  27.6 288.4 %all-to-all-done = bf16[64,56,1792]{2,1,0:T(8,128)(2,1)} async-done(((bf16[64,56,1792]{2,1,0:T(8,128)(2,1)}), bf16[64,56,1792]{2,1,0:T(8,128)(2,1)}, u32[]{:S(2)}, u32[]{:S(2)}) %all-to-all-start) | async-done | bytes 12845088 | tf_op jit(solution)/shard_map/all_to_all | solution.py:24
  316.1 7.1 convolution_multiply_fusion
  323.3 113.5 %while.34 = (s32[]{:T(128)}, f32[128,1792]{1,0:T(8,128)S(1)}, f32[128,1792]{1,0:T(8,128)S(1)}, f32[128,1792]{1,0:T(8,128)S(1)}, f32[1792]{0:T(1024)S(1)}, /*index=5*/s32[]{:T(128)}, s32[]{:T(128)}, s32[]{:T(128)}) while((s32[]{:T(128)}, f32[128,1792]{1,0:T(8,128)S(1)}, f32[128,1792]{1,0:T(8,128)S(1)}, f32[128,1792]{1,0:T(8,128)S(1)}, ...), condition=%wide.region_1.2_spmd.clone, body=%wide.region_0.1_spmd.clone.sunk | while | flops 2293767 | bytes 8264873 | solution.py:47
  326.2 2.2 collective-permute-done
  330.0 5.8 collective-permute-start
  335.8 2.2 collective-permute-done
  339.6 12.7 %collective-permute-start = (f32[128,1792]{1,0:T(8,128)}, f32[128,1792]{1,0:T(8,128)S(1)}, u32[]{:S(2)}, u32[]{:S(2)}) collective-permute-start(f32[128,1792]{1,0:T(8,128)} %get-tuple-element.455), channel_id=1, source_target_pairs={{0,32},{32,64},{64,96},{96,128},{128,160},{160,192},{192,224},{1,3... | collective-permute-start | bytes 2752520 | tf_op jit(solution)/shard_map/while/body/eval_jaxpr/ppermute | solution.py:12
  352.3 2.2 collective-permute-done
  356.0 12.7 %collective-permute-start = (f32[128,1792]{1,0:T(8,128)}, f32[128,1792]{1,0:T(8,128)S(1)}, u32[]{:S(2)}, u32[]{:S(2)}) collective-permute-start(f32[128,1792]{1,0:T(8,128)} %get-tuple-element.455), channel_id=1, source_target_pairs={{0,32},{32,64},{64,96},{96,128},{128,160},{160,192},{192,224},{1,3... | collective-permute-start | bytes 2752520 | tf_op jit(solution)/shard_map/while/body/eval_jaxpr/ppermute | solution.py:12
  368.7 2.2 collective-permute-done
  372.5 12.7 %collective-permute-start = (f32[128,1792]{1,0:T(8,128)}, f32[128,1792]{1,0:T(8,128)S(1)}, u32[]{:S(2)}, u32[]{:S(2)}) collective-permute-start(f32[128,1792]{1,0:T(8,128)} %get-tuple-element.455), channel_id=1, source_target_pairs={{0,32},{32,64},{64,96},{96,128},{128,160},{160,192},{192,224},{1,3... | collective-permute-start | bytes 2752520 | tf_op jit(solution)/shard_map/while/body/eval_jaxpr/ppermute | solution.py:12
  385.2 2.2 collective-permute-done
  389.0 12.7 %collective-permute-start = (f32[128,1792]{1,0:T(8,128)}, f32[128,1792]{1,0:T(8,128)S(1)}, u32[]{:S(2)}, u32[]{:S(2)}) collective-permute-start(f32[128,1792]{1,0:T(8,128)} %get-tuple-element.455), channel_id=1, source_target_pairs={{0,32},{32,64},{64,96},{96,128},{128,160},{160,192},{192,224},{1,3... | collective-permute-start | bytes 2752520 | tf_op jit(solution)/shard_map/while/body/eval_jaxpr/ppermute | solution.py:12
  401.6 2.2 collective-permute-done
  405.4 12.7 %collective-permute-start = (f32[128,1792]{1,0:T(8,128)}, f32[128,1792]{1,0:T(8,128)S(1)}, u32[]{:S(2)}, u32[]{:S(2)}) collective-permute-start(f32[128,1792]{1,0:T(8,128)} %get-tuple-element.455), channel_id=1, source_target_pairs={{0,32},{32,64},{64,96},{96,128},{128,160},{160,192},{192,224},{1,3... | collective-permute-start | bytes 2752520 | tf_op jit(solution)/shard_map/while/body/eval_jaxpr/ppermute | solution.py:12
  418.1 2.2 collective-permute-done
  421.9 12.7 %collective-permute-start = (f32[128,1792]{1,0:T(8,128)}, f32[128,1792]{1,0:T(8,128)S(1)}, u32[]{:S(2)}, u32[]{:S(2)}) collective-permute-start(f32[128,1792]{1,0:T(8,128)} %get-tuple-element.455), channel_id=1, source_target_pairs={{0,32},{32,64},{64,96},{96,128},{128,160},{160,192},{192,224},{1,3... | collective-permute-start | bytes 2752520 | tf_op jit(solution)/shard_map/while/body/eval_jaxpr/ppermute | solution.py:12
  434.6 2.2 collective-permute-done
  437.8 117.6 %all-reduce.2.cloned.1.call-done = f32[128,1792]{1,0:T(8,128)} async-done(((f32[128,1792]{1,0:T(8,128)}), f32[128,1792]{1,0:T(8,128)}) %all-reduce.2.cloned.1.call-update) | async-done | bytes 917520 | tf_op jit(solution)/shard_map/psum | solution.py:50
  555.5 8.4 fusion.4
  563.8 99.1 %while.35 = (s32[]{:T(128)}, f32[128,1792]{1,0:T(8,128)}, f32[1792]{0:T(1024)S(1)}, f32[1792]{0:T(1024)S(1)}, f32[128,1792]{1,0:T(8,128)S(1)}, /*index=5*/f32[12...) while((s32[]{:T(128)}, f32[128,1792]{1,0:T(8,128)}, ...), condition=%wide.region_5.6_spmd.clone, body=%wide.region_3.5_spmd.clone.sunk | while | flops 4132359 | bytes 7376058 | solution.py:65
  565.6 2.5 collective-permute-done.1
  573.2 5.9 collective-permute-done.1
  584.1 8.6 collective-permute-done.1
  597.8 8.6 collective-permute-done.1
  611.4 8.6 collective-permute-done.1
  625.0 8.6 collective-permute-done.1
  638.7 8.6 collective-permute-done.1
  652.3 8.6 collective-permute-done.1
  662.9 210.8 %psum.15 = f32[1792]{0:T(1024)} all-reduce(f32[1792]{0:T(1024)S(1)} %get-tuple-element.289), channel_id=1, replica_groups=mesh['tm'=8,'mp'=4,'tok'=8] {'tm','tok'}, use_global_device_ids=true, to_apply=%region_6.7 | all-reduce | flops 1792 | bytes 14336 | tf_op jit(solution)/shard_map/psum | solution.py:68
  (55 shorter events, 53.8 us)
Async XLA Ops:
  13.5 302.6 %copy-start.2 = (bf16[128,3584]{1,0:T(8,128)(2,1)S(1)}, bf16[128,3584]{1,0:T(8,128)(2,1)}, u32[]{:S(2)}) copy-start(bf16[128,3584]{1,0:T(8,128)(2,1)} %param.8) | copy-start | bytes 2752516
  13.5 302.6 %all-to-all-start = ((bf16[64,56,1792]{2,1,0:T(8,128)(2,1)}), bf16[64,56,1792]{2,1,0:T(8,128)(2,1)}, u32[]{:S(2)}, u32[]{:S(2)}) async-start(bf16[64,56,1792]{2,1,0:T(8,128)(2,1)} %stack.2), calls=%async_computation | async-start | bytes 25690112 | tf_op jit(solution)/shard_map/all_to_all | solution.py:24
  27.6 527.9 %all-reduce.2.cloned.1.call-start = ((), (), s32[]{:S(2)}) async-start(), calls=%async_computation.1 | async-start | bytes 1835008 | tf_op jit(solution)/shard_map/psum | solution.py:50
  316.1 7.2 copy-start.3
  324.9 3.6 collective-permute-start
  330.0 8.1 collective-permute-start
  339.6 14.9 %collective-permute-start = (f32[128,1792]{1,0:T(8,128)}, f32[128,1792]{1,0:T(8,128)S(1)}, u32[]{:S(2)}, u32[]{:S(2)}) collective-permute-start(f32[128,1792]{1,0:T(8,128)} %get-tuple-element.455), channel_id=1, source_target_pairs={{0,32},{32,64},{64,96},{96,128},{128,160},{160,192},{192,224},{1,3... | collective-permute-start | bytes 2752520 | tf_op jit(solution)/shard_map/while/body/eval_jaxpr/ppermute | solution.py:12
  356.0 14.9 %collective-permute-start = (f32[128,1792]{1,0:T(8,128)}, f32[128,1792]{1,0:T(8,128)S(1)}, u32[]{:S(2)}, u32[]{:S(2)}) collective-permute-start(f32[128,1792]{1,0:T(8,128)} %get-tuple-element.455), channel_id=1, source_target_pairs={{0,32},{32,64},{64,96},{96,128},{128,160},{160,192},{192,224},{1,3... | collective-permute-start | bytes 2752520 | tf_op jit(solution)/shard_map/while/body/eval_jaxpr/ppermute | solution.py:12
  372.5 14.9 %collective-permute-start = (f32[128,1792]{1,0:T(8,128)}, f32[128,1792]{1,0:T(8,128)S(1)}, u32[]{:S(2)}, u32[]{:S(2)}) collective-permute-start(f32[128,1792]{1,0:T(8,128)} %get-tuple-element.455), channel_id=1, source_target_pairs={{0,32},{32,64},{64,96},{96,128},{128,160},{160,192},{192,224},{1,3... | collective-permute-start | bytes 2752520 | tf_op jit(solution)/shard_map/while/body/eval_jaxpr/ppermute | solution.py:12
  389.0 14.9 %collective-permute-start = (f32[128,1792]{1,0:T(8,128)}, f32[128,1792]{1,0:T(8,128)S(1)}, u32[]{:S(2)}, u32[]{:S(2)}) collective-permute-start(f32[128,1792]{1,0:T(8,128)} %get-tuple-element.455), channel_id=1, source_target_pairs={{0,32},{32,64},{64,96},{96,128},{128,160},{160,192},{192,224},{1,3... | collective-permute-start | bytes 2752520 | tf_op jit(solution)/shard_map/while/body/eval_jaxpr/ppermute | solution.py:12
  405.4 14.9 %collective-permute-start = (f32[128,1792]{1,0:T(8,128)}, f32[128,1792]{1,0:T(8,128)S(1)}, u32[]{:S(2)}, u32[]{:S(2)}) collective-permute-start(f32[128,1792]{1,0:T(8,128)} %get-tuple-element.455), channel_id=1, source_target_pairs={{0,32},{32,64},{64,96},{96,128},{128,160},{160,192},{192,224},{1,3... | collective-permute-start | bytes 2752520 | tf_op jit(solution)/shard_map/while/body/eval_jaxpr/ppermute | solution.py:12
  421.9 14.9 %collective-permute-start = (f32[128,1792]{1,0:T(8,128)}, f32[128,1792]{1,0:T(8,128)S(1)}, u32[]{:S(2)}, u32[]{:S(2)}) collective-permute-start(f32[128,1792]{1,0:T(8,128)} %get-tuple-element.455), channel_id=1, source_target_pairs={{0,32},{32,64},{64,96},{96,128},{128,160},{160,192},{192,224},{1,3... | collective-permute-start | bytes 2752520 | tf_op jit(solution)/shard_map/while/body/eval_jaxpr/ppermute | solution.py:12
  436.8 1.0 copy-start
  437.8 126.0 %copy-start.1 = (f32[128,1792]{1,0:T(8,128)S(1)}, f32[128,1792]{1,0:T(8,128)}, u32[]{:S(2)}) copy-start(f32[128,1792]{1,0:T(8,128)} %copy-done) | copy-start | bytes 2752516
  564.3 3.8 collective-permute-start.1
  571.9 7.2 collective-permute-start.1
  582.8 9.9 %collective-permute-start.1 = (bf16[128,1792]{1,0:T(8,128)(2,1)S(1)}, bf16[128,1792]{1,0:T(8,128)(2,1)}, u32[]{:S(2)}, u32[]{:S(2)}) collective-permute-start(bf16[128,1792]{1,0:T(8,128)(2,1)S(1)} %get-tuple-element.465), channel_id=1, source_target_pairs={{32,0},{64,32},{96,64},{128,96},{160,128},{192,160},{224,192},{33,... | collective-permute-start | bytes 1376264 | tf_op jit(solution)/shard_map/while/body/eval_jaxpr/ppermute | solution.py:12
  596.5 9.9 %collective-permute-start.1 = (bf16[128,1792]{1,0:T(8,128)(2,1)S(1)}, bf16[128,1792]{1,0:T(8,128)(2,1)}, u32[]{:S(2)}, u32[]{:S(2)}) collective-permute-start(bf16[128,1792]{1,0:T(8,128)(2,1)S(1)} %get-tuple-element.465), channel_id=1, source_target_pairs={{32,0},{64,32},{96,64},{128,96},{160,128},{192,160},{224,192},{33,... | collective-permute-start | bytes 1376264 | tf_op jit(solution)/shard_map/while/body/eval_jaxpr/ppermute | solution.py:12
  610.1 9.9 %collective-permute-start.1 = (bf16[128,1792]{1,0:T(8,128)(2,1)S(1)}, bf16[128,1792]{1,0:T(8,128)(2,1)}, u32[]{:S(2)}, u32[]{:S(2)}) collective-permute-start(bf16[128,1792]{1,0:T(8,128)(2,1)S(1)} %get-tuple-element.465), channel_id=1, source_target_pairs={{32,0},{64,32},{96,64},{128,96},{160,128},{192,160},{224,192},{33,... | collective-permute-start | bytes 1376264 | tf_op jit(solution)/shard_map/while/body/eval_jaxpr/ppermute | solution.py:12
  623.7 9.9 %collective-permute-start.1 = (bf16[128,1792]{1,0:T(8,128)(2,1)S(1)}, bf16[128,1792]{1,0:T(8,128)(2,1)}, u32[]{:S(2)}, u32[]{:S(2)}) collective-permute-start(bf16[128,1792]{1,0:T(8,128)(2,1)S(1)} %get-tuple-element.465), channel_id=1, source_target_pairs={{32,0},{64,32},{96,64},{128,96},{160,128},{192,160},{224,192},{33,... | collective-permute-start | bytes 1376264 | tf_op jit(solution)/shard_map/while/body/eval_jaxpr/ppermute | solution.py:12
  637.3 9.9 %collective-permute-start.1 = (bf16[128,1792]{1,0:T(8,128)(2,1)S(1)}, bf16[128,1792]{1,0:T(8,128)(2,1)}, u32[]{:S(2)}, u32[]{:S(2)}) collective-permute-start(bf16[128,1792]{1,0:T(8,128)(2,1)S(1)} %get-tuple-element.465), channel_id=1, source_target_pairs={{32,0},{64,32},{96,64},{128,96},{160,128},{192,160},{224,192},{33,... | collective-permute-start | bytes 1376264 | tf_op jit(solution)/shard_map/while/body/eval_jaxpr/ppermute | solution.py:12
  651.0 9.9 %collective-permute-start.1 = (bf16[128,1792]{1,0:T(8,128)(2,1)S(1)}, bf16[128,1792]{1,0:T(8,128)(2,1)}, u32[]{:S(2)}, u32[]{:S(2)}) collective-permute-start(bf16[128,1792]{1,0:T(8,128)(2,1)S(1)} %get-tuple-element.465), channel_id=1, source_target_pairs={{32,0},{64,32},{96,64},{128,96},{160,128},{192,160},{224,192},{33,... | collective-permute-start | bytes 1376264 | tf_op jit(solution)/shard_map/while/body/eval_jaxpr/ppermute | solution.py:12
Sparse Core Ops, SparseCore 0:
  437.9 117.4 all-reduce.1
